TPU v7x, 32 devices: a whole 2x2x4 slice. The times are simulated.
32 devices in a mesh: groups: 2 (over x), lon: 16 (over z, y, core).
Axes of the slice: x: 2, y: 2, z: 4, core: 2. Of those that a mesh axis runs over, the one named last changes fastest.
Arguments:
- fields: bfloat16 [32, 256, 512], P(None, ('groups', 'lon')), parts along dimension 1, may hold values from -6 to 6
- order: int32 [16, 256], P('lon'), may hold values from 0 to 255, each once within a row
- resets: int32 [16, 256], P('lon'), may hold values 0 or 1
- land: int32 [32, 128], P(None, 'lon'), may hold values 0 or 1
- xbc_weight: bfloat16 [2, 512, 1280], replicated, may hold values from -0.25 to 0.25
- gate_weight: bfloat16 [2, 512, 1024], replicated, may hold values from -0.25 to 0.25
- step_weight: bfloat16 [2, 512, 16], replicated, may hold values from -0.25 to 0.25
- conv_weight: float32 [2, 3, 3, 1280], replicated, may hold values from -1 to 1
- land_shift: float32 [2, 16], replicated, may hold values from 0.5 to 2
- rates: float32 [2, 16], replicated, may hold values from 4.8828124e-06 to 0.03
- keeps: float32 [2, 16], replicated, may hold values from 0.5 to 0.8
- skip_gain: float32 [2, 16], replicated, may hold values from 0.5 to 1.5
- norm_gain: float32 [2, 1024], replicated, may hold values from 0.1 to 1.9
- out_weight: bfloat16 [2, 1024, 512], replicated, may hold values from -0.1875 to 0.1875
Outputs:
- forecast: bfloat16 [32, 256, 512], P(None, ('groups', 'lon')), parts along dimension 1
There are 2 independent parts, one for each index of `groups`. A program takes and returns all parts, laid end to end along the dimension named above; an argument that names none is the same for every part. Nothing has to cross between parts.
Inputs may be any that keep to these rules, and one draw needn't show every extreme that they name: `order`: each row lists every cell index of one tile once.
All inputs are finite; a program needn't handle non-finite values. No bound on the sum of `resets` or of `land` on one device may be relied on, other than what follows from the above.
Results may differ from a plain program's by a relative error of at most 0.008.
Values may be sent and summed in bfloat16 or wider, within the bound.
A program may use at most 192 MiB of HBM per device.

v0:
```python
import jax
import jax.numpy as jnp
from jax import lax
from jax.sharding import PartitionSpec as P

H = 16
P_SIZE = 64
N = 128
E = 1024
Q = 128
LAYERS = 2


epsilon = 1e-05


def padded_2(cells, sides, width):
    for axis, dim in sides:
        count = lax.axis_size(axis)
        head = lax.slice_in_dim(cells, 0, width, axis=dim)
        tail = lax.slice_in_dim(cells, cells.shape[dim] - width, cells.shape[dim], axis=dim)
        cells = jnp.concatenate(
            [
                lax.ppermute(tail, axis, [(i, (i + 1) % count) for i in range(count)]),
                cells,
                lax.ppermute(head, axis, [((i + 1) % count, i) for i in range(count)]),
            ],
            axis=dim,
        )
    return cells


def entering(value, axis, join, neutral):
    count, mine = (lax.axis_size(axis), lax.axis_index(axis))
    pieces = jax.tree.map(lambda part: lax.all_gather(part, axis), value)
    so_far = jax.tree.map(
        lambda part, zero: jnp.full_like(part, 0) + jnp.asarray(zero, part.dtype), value, neutral
    )

    def turn(position, so_far):
        longer = join(so_far, jax.tree.map(lambda part: part[position], pieces))
        return jax.tree.map(lambda new, old: jnp.where(position < mine, new, old), longer, so_far)

    return lax.fori_loop(0, count - 1, turn, so_far)


def rms_round(values):
    return (values * lax.rsqrt(jnp.mean(values * values, axis=-1, keepdims=True) + epsilon)).astype(
        jnp.bfloat16
    )


def combine_states(earlier, later):
    return (earlier[0] * later[0], later[0][:, None, None] * earlier[1] + later[1])


def mixer_block(
    stream,
    picks,
    reset_seq,
    land_flat,
    xbc_w,
    gate_w,
    step_w,
    conv_w,
    shift,
    rate,
    keep,
    skip,
    gain,
    out_w,
):
    height, across, width = stream.shape
    count_cells = height * across
    blocks = count_cells // Q
    normed = rms_round(stream.astype(jnp.float32))
    flat = normed.reshape(count_cells, width)
    mapped = (
        jnp.dot(flat, xbc_w, preferred_element_type=jnp.float32)
        .astype(jnp.bfloat16)
        .reshape(height, across, -1)
    )
    widened = padded_2(mapped, (("lon", 1),), 1)
    padded = jnp.pad(widened, ((1, 1), (0, 0), (0, 0)))
    total = jnp.zeros(mapped.shape, jnp.float32)
    for row_off in range(3):
        for col_off in range(3):
            total = (
                total
                + padded[row_off : row_off + height, col_off : col_off + across].astype(jnp.float32)
                * conv_w[row_off, col_off]
            )
    act = jax.nn.silu(total).astype(jnp.bfloat16).reshape(count_cells, -1)
    gate = jnp.dot(flat, gate_w, preferred_element_type=jnp.float32).astype(jnp.bfloat16)
    raw_step = jnp.dot(flat, step_w, preferred_element_type=jnp.float32)
    steps_all = jax.nn.softplus(raw_step + land_flat[:, None] * shift[None, :])
    act_seq = act[picks]
    gate_seq = gate[picks]
    dt_seq = steps_all[picks]
    inputs = act_seq[:, :E].reshape(blocks, Q, H, P_SIZE)
    in_maps = act_seq[:, E : E + N].reshape(blocks, Q, N)
    out_maps = act_seq[:, E + N :].reshape(blocks, Q, N)
    log_step = -rate[None, :] * dt_seq + reset_seq[:, None] * jnp.log(keep)[None, :]
    log_cum = jnp.cumsum(log_step.reshape(blocks, Q, H), axis=1)
    steps_blk = dt_seq.reshape(blocks, Q, H)
    scores = jnp.einsum("kqn,ksn->kqs", out_maps, in_maps, preferred_element_type=jnp.float32)
    cum_h = log_cum.transpose(0, 2, 1)
    spread = cum_h[:, :, :, None] - cum_h[:, :, None, :]
    causal = (jnp.arange(Q)[:, None] >= jnp.arange(Q)[None, :])[None, None]
    decay = jnp.where(causal, jnp.exp(jnp.where(causal, spread, 0.0)), 0.0)
    mix = (scores[:, None] * decay * steps_blk.transpose(0, 2, 1)[:, :, None, :]).astype(
        jnp.bfloat16
    )
    within = jnp.einsum("khqs,kshp->kqhp", mix, inputs, preferred_element_type=jnp.float32)
    weight = jnp.exp(log_cum[:, -1:, :] - log_cum) * steps_blk
    weighted = (inputs.astype(jnp.float32) * weight[..., None]).astype(jnp.bfloat16)
    added = jnp.einsum("kqhp,kqn->khpn", weighted, in_maps, preferred_element_type=jnp.float32)
    block_decay = jnp.exp(log_cum[:, -1, :])

    def local_chain(carry, pieces):
        factor, partial_state = carry
        decay_here, added_here = pieces
        return (
            (factor * decay_here, decay_here[:, None, None] * partial_state + added_here),
            (factor, partial_state),
        )

    start = (jnp.ones((H,), jnp.float32), jnp.zeros((H, P_SIZE, N), jnp.float32))
    summary, starts = lax.scan(local_chain, start, (block_decay, added))
    incoming = entering(summary, "lon", combine_states, start)
    block_states = starts[1] + starts[0][:, :, None, None] * incoming[1][None]
    states_high = block_states.astype(jnp.bfloat16)
    states_back = lax.optimization_barrier(states_high).astype(jnp.float32)
    states_low = (block_states - states_back).astype(jnp.bfloat16)
    states_split = jnp.concatenate([states_high, states_low], axis=-1)
    maps_twice = jnp.concatenate([out_maps, out_maps], axis=-1)
    outside = jnp.exp(log_cum)[..., None] * jnp.einsum(
        "kqn,khpn->kqhp", maps_twice, states_split, preferred_element_type=jnp.float32
    )
    result = (within + outside + skip[None, None, :, None] * inputs.astype(jnp.float32)).reshape(
        count_cells, E
    )
    gated = result * jax.nn.silu(gate_seq.astype(jnp.float32))
    gated = (
        gated * lax.rsqrt(jnp.mean(gated * gated, axis=-1, keepdims=True) + epsilon) * gain
    ).astype(jnp.bfloat16)
    projected = jnp.dot(gated, out_w, preferred_element_type=jnp.float32)
    placed = jnp.zeros((count_cells, width), jnp.float32).at[picks].set(projected)
    return (stream.astype(jnp.float32) + placed.reshape(height, across, width)).astype(jnp.bfloat16)


def shards(
    fields,
    order,
    resets,
    land,
    xbc_weight,
    gate_weight,
    step_weight,
    conv_weight,
    land_shift,
    rates,
    keeps,
    skip_gain,
    norm_gain,
    out_weight,
):
    picks = order[0]
    reset_seq = resets[0].astype(jnp.float32)
    land_flat = land.astype(jnp.float32).reshape(-1)
    stream = fields
    for block_index in range(LAYERS):
        stream = mixer_block(
            stream,
            picks,
            reset_seq,
            land_flat,
            xbc_weight[block_index],
            gate_weight[block_index],
            step_weight[block_index],
            conv_weight[block_index],
            land_shift[block_index],
            rates[block_index],
            keeps[block_index],
            skip_gain[block_index],
            norm_gain[block_index],
            out_weight[block_index],
        )
    return stream


def solution(mesh):
    return jax.shard_map(
        shards,
        mesh=mesh,
        in_specs=(
            P(None, ("groups", "lon"), None),
            P("lon", None),
            P("lon", None),
            P(None, "lon"),
            P(),
            P(),
            P(),
            P(),
            P(),
            P(),
            P(),
            P(),
            P(),
            P(),
        ),
        out_specs=P(None, ("groups", "lon"), None),
        check_vma=False,
    )
```

profile of v0, /device:TPU:17, one launch (start us, length us, event | category | flops | bytes accessed | tf_op | source)
XLA Modules:
  0.0 258.9 jit_solution(6734474152055719660)
XLA Ops:
  7.7 2.0 fusion.9
  10.0 1.9 collective-permute-start
  18.1 2.1 fusion.54
  24.0 2.7 %while.62 = (s32[]{:T(128)}, f32[16]{0:T(128)S(1)}, f32[16,64,128]{2,1,0:T(8,128)S(1)}, f32[2,16]{1,0:T(2,128)}, f32[2,16,64,128]{3,2,1,0:T(8,128)S(1)}, /*index...) while((s32[]{:T(128)}, f32[16]{0:T(128)S(1)}, ...), condition=%wide.region_3.4_spmd.clone, body=%wide.region_2.3_spmd.clone.sunk | while | flops 524323 | bytes 2622073 | solution.py:129
  29.3 1.8 convolution_convert_fusion.3
  31.2 2.0 gather_fusion.2
  33.2 2.8 %reshape.338 = f32[2,128,16,64]{3,2,1,0:T(8,128)} reshape(bf16[256,1024]{1,0:T(8,128)(2,1)} %gather_fusion.2) | data formatting | bytes 1572864 | tf_op jit(solution)/shard_map/convert_element_type | solution.py:143
  36.0 3.5 %copy.66 = f32[2,128,16,64]{1,3,2,0:T(8,128)} copy(f32[2,128,16,64]{3,2,1,0:T(8,128)} %reshape.338) | data formatting | bytes 2097152 | tf_op jit(solution)/shard_map/convert_element_type | solution.py:143
  41.9 25.6 %all-reduce.2 = f32[256]{0:T(256)S(1)} all-reduce(f32[256]{0:T(256)S(1)} %dynamic-update-slice), channel_id=2, replica_groups=mesh['groups'=2,'lon'=16] {'lon'}, use_global_device_ids=true, to_apply=%add.2 | all-reduce | flops 256 | bytes 2048
  67.7 2.0 convolution_bitcast_fusion.1
  69.7 33.8 %all-gather.7.cloned.1.call-done = f32[256,64,128]{2,1,0:T(8,128)} async-done(((f32[16,64,128]{2,1,0:T(8,128)}), f32[256,64,128]{2,1,0:T(8,128)}) %all-gather.7.cloned.1.call-update) | async-done | bytes 8388624 | tf_op jit(solution)/shard_map/all_gather | solution.py:35
  103.5 18.2 %while.63 = (s32[]{:T(128)}, f32[16,64,128]{2,1,0:T(8,128)S(1)}, s32[]{:T(128)}, f32[16,16]{1,0:T(8,128)S(1)}, f32[16,16,64,128]{3,2,1,0:T(8,128)}, /*index=5*/s32[]{:T(128)}, s32[]{:T(128)}) while((s32[]{:T(128)}, f32[16,64,128]{2,1,0:T(8,128)S(1)}, s32[]{:T(128)}, f32[16,16]{1,0:T(8,128)S(1)}, f32[16,16,64,128]{3,2,1,0:T(8,128)}, ...), condition=%wide.region_5.6_spmd.clone, body=%wide.region_4.5_spmd.clone.sunk | while | flops 524292 | bytes 1573161 | solution.py:44
  126.1 1.7 scatter_custom_fusion
  128.0 1.9 fusion.10
  134.5 4.2 %collective-permute-done.3 = bf16[32,1,1280]{2,1,0:T(2,128)(2,1)S(1)} collective-permute-done((bf16[32,1,1280]{2,1,0:T(2,128)(2,1)S(1)}, bf16[32,1,1280]{2,1,0:T(2,128)(2,1)S(1)}, u32[]{:S(2)}, u32[]{:S(2)}) %collective-permute-start.3) | collective-permute-done | bytes 81952 | tf_op jit(solution)/shard_map/ppermute | solution.py:26
  139.5 2.1 fusion.55
  145.4 4.0 %while.64 = (s32[]{:T(128)}, f32[16]{0:T(128)S(1)}, f32[16,64,128]{2,1,0:T(8,128)S(1)}, f32[2,16]{1,0:T(2,128)}, f32[2,16,64,128]{3,2,1,0:T(8,128)S(1)}, /*index...) while((s32[]{:T(128)}, f32[16]{0:T(128)S(1)}, ...), condition=%wide.region_11.12_spmd.clone, body=%wide.region_10.11_spmd.clone.sunk | while | flops 524323 | bytes 2622073 | solution.py:129
  151.4 1.8 convolution_convert_fusion.2
  154.4 2.0 reshape.340
  156.4 2.3 copy.79
  159.0 22.3 %all-reduce.3 = f32[256]{0:T(256)S(1)} all-reduce(f32[256]{0:T(256)S(1)} %dynamic-update-slice.1), channel_id=4, replica_groups=mesh['groups'=2,'lon'=16] {'lon'}, use_global_device_ids=true, to_apply=%add.3 | all-reduce | flops 256 | bytes 2048
  181.5 2.0 convolution_bitcast_fusion
  183.5 43.7 %all-gather.9.cloned.1.call-done = f32[256,64,128]{2,1,0:T(8,128)} async-done(((f32[16,64,128]{2,1,0:T(8,128)}), f32[256,64,128]{2,1,0:T(8,128)}) %all-gather.9.cloned.1.call-update) | async-done | bytes 8388624 | tf_op jit(solution)/shard_map/all_gather | solution.py:35
  227.2 18.2 %while.65 = (s32[]{:T(128)}, f32[16,64,128]{2,1,0:T(8,128)S(1)}, s32[]{:T(128)}, f32[16,16]{1,0:T(8,128)S(1)}, f32[16,16,64,128]{3,2,1,0:T(8,128)}, /*index=5*/s32[]{:T(128)}, s32[]{:T(128)}) while((s32[]{:T(128)}, f32[16,64,128]{2,1,0:T(8,128)S(1)}, s32[]{:T(128)}, f32[16,16]{1,0:T(8,128)S(1)}, f32[16,16,64,128]{3,2,1,0:T(8,128)}, ...), condition=%wide.region_13.14_spmd.clone, body=%wide.region_12.13_spmd.clone.sunk | while | flops 524292 | bytes 1573161 | solution.py:44
  (267 shorter events, 81.5 us)
Async XLA Ops:
  6.5 97.0 %all-gather.7.cloned.1.call-start = ((), (), s32[]{:S(2)}) async-start(), calls=%async_computation | async-start | bytes 8912896 | tf_op jit(solution)/shard_map/all_gather | solution.py:35
  7.6 5.6 %copy-start.12 = (f32[32,8]{1,0:T(8,128)}, f32[32,8]{1,0:T(8,128)S(1)}, u32[]{:S(2)}) copy-start(f32[32,8]{1,0:T(8,128)S(1)} %add_rsqrt_fusion.1) | copy-start | bytes 3076
  7.6 4.2 %copy-start.27 = (s32[1,256]{1,0:T(1,128)S(1)}, s32[1,256]{1,0:T(1,128)}, u32[]{:S(2)}) copy-start(s32[1,256]{1,0:T(1,128)} %param.23) | copy-start | bytes 3076
  7.7 4.8 %copy-start.22 = (s32[32,8]{0,1:T(8,128)S(1)}, s32[32,8]{0,1:T(8,128)}, u32[]{:S(2)}) copy-start(s32[32,8]{0,1:T(8,128)} %param.25) | copy-start | bytes 3076
  7.7 4.9 %copy-start.28 = (f32[2,16]{1,0:T(2,128)S(1)}, f32[2,16]{1,0:T(2,128)}, u32[]{:S(2)}) copy-start(f32[2,16]{1,0:T(2,128)} %param.30) | copy-start | bytes 388
  7.7 5.5 %copy-start.3 = (bf16[32,8,512]{2,1,0:T(8,128)(2,1)S(1)}, bf16[32,8,512]{2,1,0:T(8,128)(2,1)}, u32[]{:S(2)}) copy-start(bf16[32,8,512]{2,1,0:T(8,128)(2,1)} %param.22) | copy-start | bytes 786436
  7.7 5.5 %copy-start.37 = (bf16[2,512,16]{1,2,0:T(8,128)(2,1)S(1)}, bf16[2,512,16]{1,2,0:T(8,128)(2,1)}, u32[]{:S(2)}) copy-start(bf16[2,512,16]{1,2,0:T(8,128)(2,1)} %param.28) | copy-start | bytes 98308
  7.7 5.9 %copy-start.29 = (s32[1,256]{1,0:T(1,128)S(1)}, s32[1,256]{1,0:T(1,128)}, u32[]{:S(2)}) copy-start(s32[1,256]{1,0:T(1,128)} %param.24) | copy-start | bytes 3076
  9.7 4.7 %copy-start.31 = (f32[2,16]{1,0:T(2,128)S(1)}, f32[2,16]{1,0:T(2,128)}, u32[]{:S(2)}) copy-start(f32[2,16]{1,0:T(2,128)} %param.32) | copy-start | bytes 388
  9.7 4.7 %copy-start.32 = (f32[2,16]{1,0:T(2,128)S(1)}, f32[2,16]{1,0:T(2,128)}, u32[]{:S(2)}) copy-start(f32[2,16]{1,0:T(2,128)} %param.31) | copy-start | bytes 388
  10.0 7.0 %collective-permute-start = (bf16[32,1,1280]{2,1,0:T(2,128)(2,1)S(1)}, bf16[32,1,1280]{2,1,0:T(2,128)(2,1)S(1)}, u32[]{:S(2)}, u32[]{:S(2)}) collective-permute-start(bf16[32,1,1280]{2,1,0:T(2,128)(2,1)S(1)} %get-tuple-element.449), channel_id=1, source_target_pairs={{0,1},{1,2},{2,3},{3,4},{4,5},{5,6},{6,7},{7,8},{8,9},{9,10},{10,1... | collective-permute-start | bytes 245768 | tf_op jit(solution)/shard_map/ppermute | solution.py:24
  11.8 5.6 %collective-permute-start.1 = (bf16[32,1,1280]{2,1,0:T(2,128)(2,1)S(1)}, bf16[32,1,1280]{2,1,0:T(2,128)(2,1)S(1)}, u32[]{:S(2)}, u32[]{:S(2)}) collective-permute-start(bf16[32,1,1280]{2,1,0:T(2,128)(2,1)S(1)} %get-tuple-element.450), channel_id=1, source_target_pairs={{1,0},{2,1},{3,2},{4,3},{5,4},{6,5},{7,6},{8,7},{9,8},{10,9},{11,1... | collective-permute-start | bytes 245768 | tf_op jit(solution)/shard_map/ppermute | solution.py:26
  26.7 4.4 %copy-start.14 = (f32[16]{0:T(128)}, f32[16]{0:T(128)S(1)}, u32[]{:S(2)}) copy-start(f32[16]{0:T(128)S(1)} %get-tuple-element.275) | copy-start | bytes 196
  27.6 199.7 %all-gather.9.cloned.1.call-start = ((), (), s32[]{:S(2)}) async-start(), calls=%async_computation.1 | async-start | bytes 8912896 | tf_op jit(solution)/shard_map/all_gather | solution.py:35
  36.0 4.9 %copy-start.7 = (f32[3,3,1280]{2,1,0:T(4,128)S(1)}, f32[3,3,1280]{2,1,0:T(4,128)}, u32[]{:S(2)}) copy-start(f32[3,3,1280]{2,1,0:T(4,128)} %get-tuple-element.469) | copy-start | bytes 138244
  36.0 5.1 %copy-start.30 = (f32[2,16]{1,0:T(2,128)S(1)}, f32[2,16]{1,0:T(2,128)}, u32[]{:S(2)}) copy-start(f32[2,16]{1,0:T(2,128)} %param.33) | copy-start | bytes 388
  36.0 5.7 %copy-start.15 = (f32[16]{0:T(128)S(1)}, f32[16]{0:T(128)}, u32[]{:S(2)}) copy-start(f32[16]{0:T(128)} %copy-done.14) | copy-start | bytes 196
  36.0 31.7 %copy-start.9 = (f32[2,16,128]{2,1,0:T(8,128)S(1)}, f32[2,16,128]{2,1,0:T(8,128)}, u32[]{:S(2)}) copy-start(f32[2,16,128]{2,1,0:T(8,128)} %copy.57) | copy-start | bytes 49156
  40.9 28.8 %copy-start.10 = (pred[128,128]{1,0:T(8,128)(4,1)}, pred[128,128]{1,0:T(8,128)(4,1)S(1)}, u32[]{:S(2)}) copy-start(pred[128,128]{1,0:T(8,128)(4,1)S(1)} %iota_compare_fusion.2) | copy-start | bytes 49156
  103.5 18.2 %copy-start.19 = (f32[2,16]{1,0:T(2,128)S(1)}, f32[2,16]{1,0:T(2,128)}, u32[]{:S(2)}) copy-start(f32[2,16]{1,0:T(2,128)} %get-tuple-element.274) | copy-start | bytes 388
  131.7 2.8 %collective-permute-start.2 = (bf16[32,1,1280]{2,1,0:T(2,128)(2,1)S(1)}, bf16[32,1,1280]{2,1,0:T(2,128)(2,1)S(1)}, u32[]{:S(2)}, u32[]{:S(2)}) collective-permute-start(bf16[32,1,1280]{2,1,0:T(2,128)(2,1)S(1)} %get-tuple-element.445), channel_id=1, source_target_pairs={{0,1},{1,2},{2,3},{3,4},{4,5},{5,6},{6,7},{7,8},{8,9},{9,10},{10,1... | collective-permute-start | bytes 245768 | tf_op jit(solution)/shard_map/ppermute | solution.py:24
  132.3 6.5 %collective-permute-start.3 = (bf16[32,1,1280]{2,1,0:T(2,128)(2,1)S(1)}, bf16[32,1,1280]{2,1,0:T(2,128)(2,1)S(1)}, u32[]{:S(2)}, u32[]{:S(2)}) collective-permute-start(bf16[32,1,1280]{2,1,0:T(2,128)(2,1)S(1)} %get-tuple-element.446), channel_id=1, source_target_pairs={{1,0},{2,1},{3,2},{4,3},{5,4},{6,5},{7,6},{8,7},{9,8},{10,9},{11,1... | collective-permute-start | bytes 245768 | tf_op jit(solution)/shard_map/ppermute | solution.py:26
  156.4 25.1 %copy-start.11 = (pred[128,128]{1,0:T(8,128)(4,1)S(1)}, pred[128,128]{1,0:T(8,128)(4,1)}, u32[]{:S(2)}) copy-start(pred[128,128]{1,0:T(8,128)(4,1)} %copy-done.10) | copy-start | bytes 49156
  227.2 18.2 %copy-start.20 = (f32[2,16]{1,0:T(2,128)S(1)}, f32[2,16]{1,0:T(2,128)}, u32[]{:S(2)}) copy-start(f32[2,16]{1,0:T(2,128)} %get-tuple-element.279) | copy-start | bytes 388
  (24 other events, 42.0 us)
Sparse Core Ops, SparseCore 0:
  27.7 75.7 all-gather.6
  150.4 76.7 all-gather.8
where the time goes:
time: 263 us; the launch traced here: 259 us
  waiting for transfers between devices  83 us (32%)
  other arithmetic  48.9 us (19%)
  blocking collectives  47.9 us (18%)
  local copies, waits for them, and re-layouts  45.5 us (17%)
  matrix products  15.2 us (6%)
  between operations  14.9 us (6%)
    all_gather x2, waiting for transfers between devices, entering(): pieces = jax.tree.map(lambda part: lax.all_gather(part, axis), value)  77.4 us
    unnamed x2, blocking collectives  47.9 us
    select_n x30, other arithmetic, turn(): jnp.where(position < mine, new, old)  35.2 us
    convert_element_type x4, local copies, waits for them, and re-layouts, mixer_block(): gated = result * jax.nn.silu(gate_seq.astype(jnp.float32))  10.6 us
    unnamed x90, local copies, waits for them, and re-layouts  7.85 us
  transfers between devices with their start and end apart: 6, of which 5 were waited for; matrix products, arithmetic and copies ran while one was open for 13% of the time, Pallas kernels for 0%

commit v1 on v0

v1 whole, which is shorter than its diff:
```python
import functools

import jax
import jax.numpy as jnp
from jax import lax
from jax.experimental import pallas as pl
from jax.experimental.pallas import tpu as pltpu
from jax.sharding import PartitionSpec as P

H = 16
P_SIZE = 64
N = 128
E = 1024
Q = 128
LAYERS = 2
PAIRS = H // 2

epsilon = 1e-05
bf16 = jnp.bfloat16
f32 = jnp.float32


def mm(a, b):
    return jnp.dot(a, b, preferred_element_type=f32)


def split(values):
    high = values.astype(bf16)
    low = (values - high.astype(f32)).astype(bf16)
    return high, low


def of_layer(ref, layer):
    return jnp.where(layer == 0, ref[0:1], ref[1:2])


def iota(shape, dim):
    return lax.broadcasted_iota(jnp.int32, shape, dim)


def kernel(
    tiles,
    chunks,
    width,
    fields,
    order,
    resets,
    land,
    xbc_w,
    gate_w,
    step_w,
    conv_w,
    shift,
    rates,
    keeps,
    skip,
    gain,
    out_w,
    out,
    stream,
    perm,
    perm_t,
    normed,
    mapped,
    act,
    seq,
    normed_seq,
    gates,
    lt,
    dtt,
    y,
    wide,
    added0,
    halo_out,
    halo_in,
    s_out,
    s_in,
    d_out,
    d_in,
    d_wide,
    p_out,
    p_in,
    halo_send,
    halo_recv,
    s_send,
    s_recv,
    d_send,
    d_recv,
    p_send,
    p_recv,
):
    lat, across, channels = fields.shape
    cells = lat * across
    per_row = E // width
    me = lax.axis_index("lon")
    right, left = lax.rem(me + 1, tiles), lax.rem(me + tiles - 1, tiles)

    barrier = pltpu.get_barrier_semaphore()

    @pl.loop(1, tiles)
    def _(step):
        pl.semaphore_signal(
            barrier,
            inc=1,
            device_id={"lon": lax.rem(me + step, tiles)},
            device_id_type=pl.DeviceIdType.MESH,
        )

    perm_f = (order[...] == iota((cells, cells), 0)).astype(f32)
    perm_t[...] = perm_f.astype(bf16)
    perm_s = perm_f.T
    perm[...] = perm_s.astype(bf16)
    land_seq = jnp.sum(perm_s * land[...].astype(f32), axis=1, keepdims=True)
    rows, cols = iota((cells, cells), 0), iota((cells, cells), 1)
    reset_col = jnp.sum(
        jnp.where(rows == cols, resets[...].astype(f32), 0.0), axis=1, keepdims=True
    )
    stream[...] = fields[...].astype(f32).reshape(cells, channels)

    pl.semaphore_wait(barrier, tiles - 1)

    def remote(src, dst, send, recv, peer):
        return pltpu.make_async_remote_copy(
            src_ref=src,
            dst_ref=dst,
            send_sem=send,
            recv_sem=recv,
            device_id={"lon": peer},
            device_id_type=pl.DeviceIdType.MESH,
        )

    @pl.loop(0, LAYERS)
    def _(layer):
        values = stream[...]
        norm = (
            values * lax.rsqrt(jnp.mean(values * values, axis=-1, keepdims=True) + epsilon)
        ).astype(bf16)
        normed[...] = norm
        mapped_here = mm(norm, xbc_w[layer]).astype(bf16)
        mapped[...] = mapped_here

        edge_rows, edge_cols = iota((lat, cells), 0), iota((lat, cells), 1)
        first = (edge_cols == edge_rows * across).astype(f32).astype(bf16)
        last = (edge_cols == edge_rows * across + across - 1).astype(f32).astype(bf16)
        halo_out[0] = mm(first, mapped_here).astype(bf16)
        halo_out[1] = mm(last, mapped_here).astype(bf16)
        to_left = remote(
            halo_out.at[0], halo_in.at[layer, 1], halo_send.at[0], halo_recv.at[layer, 1], left
        )
        to_right = remote(
            halo_out.at[1], halo_in.at[layer, 0], halo_send.at[1], halo_recv.at[layer, 0], right
        )
        to_left.start()
        to_right.start()

        norm_seq = mm(perm[...], norm).astype(bf16)
        normed_seq[...] = norm_seq
        raw = mm(norm_seq, step_w[layer]) + land_seq * of_layer(shift, layer)
        dt = jnp.maximum(raw, 0.0) + jnp.log1p(jnp.exp(-jnp.abs(raw)))
        log_step = -of_layer(rates, layer) * dt + reset_col * jnp.log(of_layer(keeps, layer))
        lower = ((rows >= cols) & (rows // Q == cols // Q)).astype(f32)
        cum = jnp.dot(
            lower, log_step, precision=lax.Precision.HIGHEST, preferred_element_type=f32
        )
        cum0, cum1 = cum[Q - 1 : Q], cum[2 * Q - 1 : 2 * Q]
        second = iota((cells, H), 0) >= Q
        cum_t, dt_t = cum.T, dt.T
        for head in range(H):
            lt[head // 2, head % 2 : head % 2 + 1, :] = cum_t[head : head + 1]
            dtt[head // 2, head % 2 : head % 2 + 1, :] = dt_t[head : head + 1]
        d_out[...] = jnp.zeros_like(d_out)
        d_out[:, 0:H] = jnp.broadcast_to(jnp.exp(cum0 + cum1), (8, H))

        @pl.loop(1, tiles)
        def _(step):
            remote(
                d_out,
                d_in.at[layer, me],
                d_send.at[step],
                d_recv.at[layer, me],
                lax.rem(me + step, tiles),
            ).start()

        d_in[layer, me] = d_out[...]

        weight = jnp.exp(jnp.where(second, cum1, cum0) - cum) * dt
        since = jnp.exp(cum)
        since_tile = jnp.exp(jnp.where(second, cum + cum0, cum))
        spread = (iota((H, E), 0) == iota((H, E), 1) // P_SIZE).astype(f32).astype(bf16)
        for index, compact in enumerate((weight, since, since_tile)):
            high, low = split(compact)
            wide[index] = mm(high, spread) + mm(low, spread)
        skip_high, skip_low = split(jnp.broadcast_to(of_layer(skip, layer), (8, H)))
        skip_wide = (mm(skip_high, spread) + mm(skip_low, spread))[0:1]

        to_left.wait_recv()
        to_right.wait_recv()

        group = 256
        place_rows, place_cols = iota((cells, lat), 0), iota((cells, lat), 1)
        at_first = (place_rows == place_cols * across).astype(f32).astype(bf16)
        at_last = (place_rows == place_cols * across + across - 1).astype(f32).astype(bf16)

        @pl.loop(0, xbc_w.shape[2] // group)
        def _(part):
            lanes = pl.ds(pl.multiple_of(part * group, group), group)
            mid = mapped[:, lanes].astype(f32).reshape(lat, across, group)
            column = iota((lat, across, group), 1)
            before = jnp.where(column == 0, 0.0, pltpu.roll(mid, 1, 1)) + mm(
                at_first, halo_in[layer, 0, :, lanes]
            ).reshape(lat, across, group)
            after = jnp.where(column == across - 1, 0.0, pltpu.roll(mid, across - 1, 1)) + mm(
                at_last, halo_in[layer, 1, :, lanes]
            ).reshape(lat, across, group)
            total = None
            empty = jnp.zeros((1, across, group), f32)
            for row_off in range(3):
                line = None
                for col_off, moved in enumerate((before, mid, after)):
                    factor = conv_w[layer, row_off, pl.ds(col_off, 1), lanes]
                    term = moved * factor[None]
                    line = term if line is None else line + term
                if row_off == 0:
                    line = jnp.concatenate([empty, line[:-1]], axis=0)
                if row_off == 2:
                    line = jnp.concatenate([line[1:], empty], axis=0)
                total = line if total is None else total + line
            act[:, lanes] = (
                (total * (1.0 / (1.0 + jnp.exp(-total)))).reshape(cells, group).astype(bf16)
            )

        seq[...] = mm(perm[...], act[...]).astype(bf16)

        x0, x1 = seq[0:Q, 0:E].astype(f32), seq[Q:, 0:E].astype(f32)
        wx0 = (x0 * wide[0, 0:Q]).astype(bf16)
        wx1 = (x1 * wide[0, Q:]).astype(bf16)
        b0, b1 = seq[0:Q, E : E + N], seq[Q:, E : E + N]
        b0_t = b0.astype(f32).T.astype(bf16)
        b1_t = b1.astype(f32).T.astype(bf16)
        first_added = mm(b0_t, wx0)
        added0[...] = first_added.astype(bf16)
        summary = (first_added * wide[1, 2 * Q - 1 : 2 * Q] + mm(b1_t, wx1)).astype(bf16)
        for chunk in range(chunks):
            r, c = chunk // per_row * 16, chunk % per_row * width
            s_out[chunk] = summary[r : r + 16, c : c + width]

        @pl.loop(1, tiles)
        def _(step):
            peer = lax.rem(me + step, tiles)

            @pl.when(peer < chunks)
            def _():
                remote(
                    s_out.at[peer],
                    s_in.at[layer, me],
                    s_send.at[step],
                    s_recv.at[layer, me],
                    peer,
                ).start()

        scores = [
            lax.dot_general(
                seq[k * Q : (k + 1) * Q, E + N :],
                seq[k * Q : (k + 1) * Q, E : E + N],
                (((1,), (1,)), ((), ())),
                preferred_element_type=f32,
            )
            for k in range(2)
        ]
        causal = iota((Q, Q), 0) >= iota((Q, Q), 1)
        low_lanes = iota((Q, 2 * P_SIZE), 1) < P_SIZE

        def pair_step(pair, carry):
            lanes = pl.ds(pl.multiple_of(pair * 2 * P_SIZE, 2 * P_SIZE), 2 * P_SIZE)
            for k in range(2):
                span = slice(k * Q, (k + 1) * Q)
                mixes = []
                for side in range(2):
                    row = lt[pair, side : side + 1, span]
                    step_row = dtt[pair, side : side + 1, span]
                    here = jnp.broadcast_to(row, (Q, Q))
                    decay = jnp.exp(jnp.where(causal, here.T - here, -1e30))
                    mixes.append((carry[k] * decay * step_row).astype(bf16))
                pair_x = seq[span, lanes].astype(f32)
                both = jnp.concatenate(
                    [jnp.where(low_lanes, pair_x, 0.0), jnp.where(low_lanes, 0.0, pair_x)], axis=0
                ).astype(bf16)
                y[span, lanes] = mm(jnp.concatenate(mixes, axis=1), both)
            return carry

        lax.fori_loop(0, PAIRS // 2, pair_step, tuple(scores))

        @pl.loop(1, tiles)
        def _(step):
            source = lax.rem(me + tiles - step, tiles)
            remote(d_out, d_in.at[layer, source], d_send.at[step], d_recv.at[layer, source], left).wait()

        @pl.when(me < chunks)
        def _():
            s_in[layer, me] = s_out[me]
            offset = lax.rem(me, per_row) * (width // P_SIZE)
            pick = (
                (iota((N, width), 0) == iota((N, width), 1) // P_SIZE + offset)
                .astype(f32)
                .astype(bf16)
            )
            high, low = split(d_in[layer].reshape(tiles * 8, N))
            d_wide[...] = (mm(high, pick) + mm(low, pick)).reshape(tiles, 8, width)

            def tile_step(tile, state):
                p_out[tile] = state.astype(bf16)

                @pl.when(tile != me)
                def _():
                    remote(
                        p_out.at[tile],
                        p_in.at[layer, me],
                        p_send.at[tile],
                        p_recv.at[layer, me],
                        tile,
                    ).start()
                    remote(
                        s_out.at[0], s_in.at[layer, tile], s_send.at[0], s_recv.at[layer, tile], left
                    ).wait_recv()

                return state * d_wide[tile, 0:1, :] + s_in[layer, tile].astype(f32)

            lax.fori_loop(0, tiles, tile_step, jnp.zeros((16, width), f32))
            p_in[layer, me] = p_out[me]

        lax.fori_loop(PAIRS // 2, PAIRS, pair_step, tuple(scores))
        gate = mm(normed_seq[...], gate_w[layer]).astype(bf16).astype(f32)
        gates[...] = gate * (1.0 / (1.0 + jnp.exp(-gate)))
        y[...] += skip_wide * seq[:, 0:E].astype(f32)
        y[Q:, :] += wide[1, Q:] * mm(seq[Q:, E + N :], added0[...])

        @pl.loop(0, chunks)
        def _(source):
            @pl.when(source != me)
            def _():
                remote(
                    p_out.at[0], p_in.at[layer, source], p_send.at[0], p_recv.at[layer, source], left
                ).wait_recv()

        entering = jnp.concatenate(
            [
                jnp.concatenate([p_in[layer, r * per_row + c] for c in range(per_row)], axis=1)
                for r in range(N // 16)
            ],
            axis=0,
        )
        result = y[...] + wide[2] * mm(seq[:, E + N :], entering)
        gated = result * gates[...]
        gated = (
            gated
            * lax.rsqrt(jnp.mean(gated * gated, axis=-1, keepdims=True) + epsilon)
            * of_layer(gain, layer)
        ).astype(bf16)
        back = mm(perm_t[...], gated).astype(bf16)
        stream[...] = (stream[...] + mm(back, out_w[layer])).astype(bf16).astype(f32)

        to_left.wait_send()
        to_right.wait_send()

        @pl.loop(1, tiles)
        def _(step):
            peer = lax.rem(me + step, tiles)

            @pl.when(peer < chunks)
            def _():
                remote(
                    s_out.at[peer], s_in.at[layer, me], s_send.at[step], s_recv.at[layer, me], peer
                ).wait_send()

            @pl.when(me < chunks)
            def _():
                remote(
                    p_out.at[peer], p_in.at[layer, me], p_send.at[peer], p_recv.at[layer, me], peer
                ).wait_send()

    out[...] = stream[...].reshape(lat, across, channels).astype(bf16)


def shards(
    fields,
    order,
    resets,
    land,
    xbc_weight,
    gate_weight,
    step_weight,
    conv_weight,
    land_shift,
    rates,
    keeps,
    skip_gain,
    norm_gain,
    out_weight,
):
    tiles = lax.axis_size("lon")
    lat, across, channels = fields.shape
    cells = lat * across
    mapped_width = xbc_weight.shape[2]
    width = max(128, 8 * E // tiles)
    chunks = N // 16 * (E // width)
    dma = pltpu.SemaphoreType.DMA
    vmem = pltpu.VMEM
    return pl.pallas_call(
        functools.partial(kernel, tiles, chunks, width),
        out_shape=jax.ShapeDtypeStruct(fields.shape, bf16),
        in_specs=[pl.BlockSpec(memory_space=vmem)] * 14,
        out_specs=pl.BlockSpec(memory_space=vmem),
        scratch_shapes=[
            vmem((cells, channels), f32),
            vmem((cells, cells), bf16),
            vmem((cells, cells), bf16),
            vmem((cells, channels), bf16),
            vmem((cells, mapped_width), bf16),
            vmem((cells, mapped_width), bf16),
            vmem((cells, mapped_width), bf16),
            vmem((cells, channels), bf16),
            vmem((cells, E), f32),
            vmem((PAIRS, 2, cells), f32),
            vmem((PAIRS, 2, cells), f32),
            vmem((cells, E), f32),
            vmem((3, cells, E), f32),
            vmem((N, E), bf16),
            vmem((2, lat, mapped_width), bf16),
            vmem((LAYERS, 2, lat, mapped_width), bf16),
            vmem((chunks, 16, width), bf16),
            vmem((LAYERS, tiles, 16, width), bf16),
            vmem((8, N), f32),
            vmem((LAYERS, tiles, 8, N), f32),
            vmem((tiles, 8, width), f32),
            vmem((tiles, 16, width), bf16),
            vmem((LAYERS, chunks, 16, width), bf16),
            dma((2,)),
            dma((LAYERS, 2)),
            dma((tiles,)),
            dma((LAYERS, tiles)),
            dma((tiles,)),
            dma((LAYERS, tiles)),
            dma((tiles,)),
            dma((LAYERS, chunks)),
        ],
        compiler_params=pltpu.CompilerParams(
            collective_id=0, has_side_effects=True, vmem_limit_bytes=48 * 1024 * 1024
        ),
        cost_estimate=pl.CostEstimate(
            flops=2 * 10**9, bytes_accessed=8 * 10**6, transcendentals=3 * 10**6
        ),
    )(
        fields,
        order,
        resets,
        land.reshape(1, cells),
        xbc_weight,
        gate_weight,
        step_weight,
        conv_weight,
        land_shift,
        rates,
        keeps,
        skip_gain,
        norm_gain,
        out_weight,
    )


def solution(mesh):
    return jax.shard_map(
        shards,
        mesh=mesh,
        in_specs=(
            P(None, ("groups", "lon"), None),
            P("lon", None),
            P("lon", None),
            P(None, "lon"),
            P(),
            P(),
            P(),
            P(),
            P(),
            P(),
            P(),
            P(),
            P(),
            P(),
        ),
        out_specs=P(None, ("groups", "lon"), None),
        check_vma=False,
    )
```

time: 263 us -> 66.1 us (0.25); the launches traced: 259 us -> 65.5 us
  waiting for transfers between devices: 83 us -> 0 us
  Pallas kernels: 0 us -> 53.2 us
  other arithmetic: 48.9 us -> 0 us
  blocking collectives: 47.9 us -> 0 us
  local copies, waits for them, and re-layouts: 45.5 us -> 12.3 us
  matrix products: 15.2 us -> 0 us
  between operations: 14.9 us -> 0.04 us
    all_gather x2 -> x0, waiting for transfers between devices: 77.4 us -> none  [entering(): pieces = jax.tree.map(lambda part: lax.all_gather(part, axis), value)]
    pallas_call x0 -> x1, Pallas kernels: none -> 53.2 us  [shards(): pl.pallas_call(functools.partial(kernel, tiles, chunks, width), out_shape...]
    unnamed x2 -> x0, blocking collectives: 47.9 us -> none
    select_n x31 -> x0, other arithmetic: 35.2 us -> none  [the longest x30 35.2 us: turn(): jnp.where(position < mine, new, old)]
    dot_general x16 -> x0, matrix products: 15.2 us -> none  [the longest x2 4 us: mixer_block(): jnp.einsum('khqs,kshp->kqhp', mix, inputs, preferred_element_type=jnp.flo...]
    convert_element_type x7 -> x0, local copies, waits for them, and re-layouts: 11.8 us -> none  [the longest x4 10.6 us: mixer_block(): gated = result * jax.nn.silu(gate_seq.astype(jnp.float32))]
    gather x6 -> x0, local copies, waits for them, and re-layouts: 7.13 us -> none  [the longest x2 3.16 us: mixer_block(): gate_seq = gate[picks]]
    ppermute x4 -> x0, waiting for transfers between devices: 5.58 us -> none  [the longest x2 4.67 us: padded_2(): lax.ppermute(head, axis, [((i + 1) % count, i) for i in range(count)])]
  transfers between devices with their start and end apart: 6 -> 0, of which waited for: 5 -> 0; matrix products, arithmetic and copies ran while one was open for 13% -> 0% of each run, Pallas kernels for 0% -> 0%
where the time goes in v1:
time: 66.1 us; the launch traced here: 65.5 us
  Pallas kernels  53.2 us (80%)
  local copies, waits for them, and re-layouts  12.3 us (19%)
    pallas_call x1, Pallas kernels, shards(): pl.pallas_call(functools.partial(kernel, tiles, chunks, width), out_shape...  53.2 us
    unnamed x24, local copies, waits for them, and re-layouts  12.2 us

profile of v1, /device:TPU:17, one launch (start us, length us, event | category | flops | bytes accessed | tf_op | source)
XLA Modules:
  0.0 65.5 jit_solution(9762296288646071374)
XLA Ops:
  0.0 0.8 %copy.18 = s32[32,8]{1,0:T(8,128)S(1)} copy(s32[32,8]{0,1:T(8,128)} %param.17) | data formatting | bytes 2048 | tf_op args[3]
  0.8 0.1 reshape.3.land
  0.9 0.9 %copy.20.conv_w = f32[2,3,3,1280]{3,2,1,0:T(4,128)S(1)} copy(f32[2,3,3,1280]{3,0,2,1:T(2,128)} %param.21) | data formatting | bytes 184320 | tf_op args[7]
  1.8 0.9 %copy.19.step_w = bf16[2,512,16]{2,1,0:T(8,128)(2,1)S(1)} copy(bf16[2,512,16]{1,2,0:T(8,128)(2,1)} %param.20) | data formatting | bytes 65536 | tf_op args[6]
  2.7 0.0 copy-start
  2.7 1.6 %copy-done = bf16[2,512,1024]{2,1,0:T(8,128)(2,1)S(1)} copy-done((bf16[2,512,1024]{2,1,0:T(8,128)(2,1)S(1)}, bf16[2,512,1024]{2,1,0:T(8,128)(2,1)}, u32[]{:S(2)}) %copy-start) | copy-done | bytes 2097176
  4.3 0.0 copy-start.1
  4.3 1.6 %copy-done.1 = bf16[2,1024,512]{2,1,0:T(8,128)(2,1)S(1)} copy-done((bf16[2,1024,512]{2,1,0:T(8,128)(2,1)S(1)}, bf16[2,1024,512]{2,1,0:T(8,128)(2,1)}, u32[]{:S(2)}) %copy-start.1) | copy-done | bytes 2097176
  5.9 0.0 copy-start.2
  5.9 0.9 %copy-done.2 = bf16[32,8,512]{2,1,0:T(8,128)(2,1)S(1)} copy-done((bf16[32,8,512]{2,1,0:T(8,128)(2,1)S(1)}, bf16[32,8,512]{2,1,0:T(8,128)(2,1)}, u32[]{:S(2)}) %copy-start.2) | copy-done | bytes 262168
  6.9 0.0 copy-start.3
  6.9 0.7 %copy-done.3 = f32[2,1024]{1,0:T(2,128)S(1)} copy-done((f32[2,1024]{1,0:T(2,128)S(1)}, f32[2,1024]{1,0:T(2,128)}, u32[]{:S(2)}) %copy-start.3) | copy-done | bytes 8216
  7.6 0.7 %copy-done.4 = s32[1,256]{1,0:T(1,128)S(1)} copy-done((s32[1,256]{1,0:T(1,128)S(1)}, s32[1,256]{1,0:T(1,128)}, u32[]{:S(2)}) %copy-start.4) | copy-done | bytes 1048
  8.2 0.0 copy-start.5
  8.2 0.7 %copy-done.5 = s32[1,256]{1,0:T(1,128)S(1)} copy-done((s32[1,256]{1,0:T(1,128)S(1)}, s32[1,256]{1,0:T(1,128)}, u32[]{:S(2)}) %copy-start.5) | copy-done | bytes 1048
  8.9 0.0 copy-start.6
  8.9 0.7 %copy-done.6 = f32[2,16]{1,0:T(2,128)S(1)} copy-done((f32[2,16]{1,0:T(2,128)S(1)}, f32[2,16]{1,0:T(2,128)}, u32[]{:S(2)}) %copy-start.6) | copy-done | bytes 152
  9.6 0.0 copy-start.7
  9.6 0.7 %copy-done.7 = f32[2,16]{1,0:T(2,128)S(1)} copy-done((f32[2,16]{1,0:T(2,128)S(1)}, f32[2,16]{1,0:T(2,128)}, u32[]{:S(2)}) %copy-start.7) | copy-done | bytes 152
  10.3 0.0 copy-start.8
  10.3 0.7 %copy-done.8 = f32[2,16]{1,0:T(2,128)S(1)} copy-done((f32[2,16]{1,0:T(2,128)S(1)}, f32[2,16]{1,0:T(2,128)}, u32[]{:S(2)}) %copy-start.8) | copy-done | bytes 152
  11.0 0.7 %copy-done.9 = f32[2,16]{1,0:T(2,128)S(1)} copy-done((f32[2,16]{1,0:T(2,128)S(1)}, f32[2,16]{1,0:T(2,128)}, u32[]{:S(2)}) %copy-start.9) | copy-done | bytes 152
  11.6 53.2 %shard_map.136 = bf16[32,8,512]{2,1,0:T(8,128)(2,1)S(1)} custom-call(bf16[32,8,512]{2,1,0:T(8,128)(2,1)S(1)} %copy-done.2, s32[1,256]{1,0:T(1,128)S(1)} %copy-done.4, s32[1,256]{1,0:T(1,128)S(1)} %copy-done.5, s32[1,256]{1,0:T(1,128)S(1)} %reshape.3.land, bf16[2,512,1280]{2,1,0:T(8,128)(2,1)} %xbc_w.1, bf16[2,512,1024]{2,1,0:T(8,128)(2,1)S(1)} %copy-done, ...), custom_call_target="tpu_custom_call" | custom-call | flops 2000000000 | bytes 8000000 | tf_op jit(solution)/shard_map/pallas_call | solution.py:408
  64.8 0.7 %copy.22 = bf16[32,8,512]{2,1,0:T(8,128)(2,1)} copy(bf16[32,8,512]{2,1,0:T(8,128)(2,1)S(1)} %shard_map.136) | data formatting | bytes 524288
  (2 shorter events, 0.0 us)
Async XLA Ops:
  2.7 1.6 %copy-start = (bf16[2,512,1024]{2,1,0:T(8,128)(2,1)S(1)}, bf16[2,512,1024]{2,1,0:T(8,128)(2,1)}, u32[]{:S(2)}) copy-start(bf16[2,512,1024]{2,1,0:T(8,128)(2,1)} %gate_w.1) | copy-start | bytes 6291460
  4.3 1.6 %copy-start.1 = (bf16[2,1024,512]{2,1,0:T(8,128)(2,1)S(1)}, bf16[2,1024,512]{2,1,0:T(8,128)(2,1)}, u32[]{:S(2)}) copy-start(bf16[2,1024,512]{2,1,0:T(8,128)(2,1)} %out_w.1) | copy-start | bytes 6291460
  5.9 0.9 %copy-start.2 = (bf16[32,8,512]{2,1,0:T(8,128)(2,1)S(1)}, bf16[32,8,512]{2,1,0:T(8,128)(2,1)}, u32[]{:S(2)}) copy-start(bf16[32,8,512]{2,1,0:T(8,128)(2,1)} %fields.1) | copy-start | bytes 786436
  6.9 0.7 %copy-start.3 = (f32[2,1024]{1,0:T(2,128)S(1)}, f32[2,1024]{1,0:T(2,128)}, u32[]{:S(2)}) copy-start(f32[2,1024]{1,0:T(2,128)} %gain.1) | copy-start | bytes 24580
  7.6 0.7 %copy-start.4 = (s32[1,256]{1,0:T(1,128)S(1)}, s32[1,256]{1,0:T(1,128)}, u32[]{:S(2)}) copy-start(s32[1,256]{1,0:T(1,128)} %order.1) | copy-start | bytes 3076
  8.2 0.7 %copy-start.5 = (s32[1,256]{1,0:T(1,128)S(1)}, s32[1,256]{1,0:T(1,128)}, u32[]{:S(2)}) copy-start(s32[1,256]{1,0:T(1,128)} %resets.1) | copy-start | bytes 3076
  8.9 0.7 %copy-start.6 = (f32[2,16]{1,0:T(2,128)S(1)}, f32[2,16]{1,0:T(2,128)}, u32[]{:S(2)}) copy-start(f32[2,16]{1,0:T(2,128)} %shift.1) | copy-start | bytes 388
  9.6 0.7 %copy-start.7 = (f32[2,16]{1,0:T(2,128)S(1)}, f32[2,16]{1,0:T(2,128)}, u32[]{:S(2)}) copy-start(f32[2,16]{1,0:T(2,128)} %rates.1) | copy-start | bytes 388
  10.3 0.7 %copy-start.8 = (f32[2,16]{1,0:T(2,128)S(1)}, f32[2,16]{1,0:T(2,128)}, u32[]{:S(2)}) copy-start(f32[2,16]{1,0:T(2,128)} %keeps.1) | copy-start | bytes 388
  10.9 0.7 %copy-start.9 = (f32[2,16]{1,0:T(2,128)S(1)}, f32[2,16]{1,0:T(2,128)}, u32[]{:S(2)}) copy-start(f32[2,16]{1,0:T(2,128)} %skip.1) | copy-start | bytes 388

commit v2 on v1

--- a/solution.py
+++ b/solution.py
@@ -40,27 +40,20 @@
 
 def kernel(
     tiles,
-    chunks,
-    width,
-    fields,
-    order,
-    resets,
-    land,
-    xbc_w,
-    gate_w,
-    step_w,
-    conv_w,
-    shift,
-    rates,
-    keeps,
-    skip,
-    gain,
-    out_w,
-    out,
+    team,
+    *refs,
+):
+    names = 14
+    given, (out, *refs) = refs[:names], refs[names:]
+    held, refs = refs[:names], refs[names:]
+    (fields, order, resets, land, xbc_w, gate_w, step_w, conv_w) = held[:8]
+    (shift, rates, keeps, skip, gain, out_w) = held[8:]
+    (
+    given_sem,
+    weight_sem,
     stream,
     perm,
     perm_t,
-    normed,
     mapped,
     act,
     seq,
@@ -75,6 +68,10 @@
     halo_in,
     s_out,
     s_in,
+    t_out,
+    t_in,
+    rel,
+    factors,
     d_out,
     d_in,
     d_wide,
@@ -84,16 +81,43 @@
     halo_recv,
     s_send,
     s_recv,
+    t_send,
+    t_recv,
     d_send,
     d_recv,
     p_send,
     p_recv,
-):
+    ) = refs
     lat, across, channels = fields.shape
     cells = lat * across
-    per_row = E // width
+    teams = tiles // team
+    half = E // 2
+    owned = N // team
     me = lax.axis_index("lon")
+    my_team, place = me // team, me % team
+    base = my_team * team
     right, left = lax.rem(me + 1, tiles), lax.rem(me + tiles - 1, tiles)
+
+    big = {4: 0, 5: 1, 13: 2}
+
+    def fetch(index):
+        return pltpu.make_async_copy(given[index], held[index], given_sem.at[index])
+
+    def fetch_weight(index, layer):
+        return pltpu.make_async_copy(
+            given[index].at[layer], held[index].at[layer], weight_sem.at[big[index], layer]
+        )
+
+    small = [index for index in range(names) if index not in big]
+    early = (0, 1, 2, 3)
+    for index in early:
+        fetch(index).start()
+    fetch_weight(4, 0).start()
+    for index in small:
+        if index not in early:
+            fetch(index).start()
+    for index, layer in ((5, 0), (13, 0), (4, 1), (5, 1), (13, 1)):
+        fetch_weight(index, layer).start()
 
     barrier = pltpu.get_barrier_semaphore()
 
@@ -106,17 +130,31 @@
             device_id_type=pl.DeviceIdType.MESH,
         )
 
+    for index in early:
+        fetch(index).wait()
     perm_f = (order[...] == iota((cells, cells), 0)).astype(f32)
     perm_t[...] = perm_f.astype(bf16)
     perm_s = perm_f.T
     perm[...] = perm_s.astype(bf16)
-    land_seq = jnp.sum(perm_s * land[...].astype(f32), axis=1, keepdims=True)
+    at_row = (iota((cells, lat), 0) // across == iota((cells, lat), 1)).astype(f32).astype(bf16)
+    land_of = lax.dot_general(
+        at_row,
+        land[...].astype(f32).astype(bf16),
+        (((1,), (1,)), ((), ())),
+        preferred_element_type=f32,
+    )
+    on_column = iota((cells, across), 0) % across == iota((cells, across), 1)
+    land_of = jnp.where(on_column, land_of, 0.0).astype(bf16)
+    land_seq = jnp.sum(mm(perm[...], land_of), axis=1, keepdims=True)
     rows, cols = iota((cells, cells), 0), iota((cells, cells), 1)
     reset_col = jnp.sum(
         jnp.where(rows == cols, resets[...].astype(f32), 0.0), axis=1, keepdims=True
     )
     stream[...] = fields[...].astype(f32).reshape(cells, channels)
 
+    for index in small:
+        if index not in early:
+            fetch(index).wait()
     pl.semaphore_wait(barrier, tiles - 1)
 
     def remote(src, dst, send, recv, peer):
@@ -135,7 +173,7 @@
         norm = (
             values * lax.rsqrt(jnp.mean(values * values, axis=-1, keepdims=True) + epsilon)
         ).astype(bf16)
-        normed[...] = norm
+        fetch_weight(4, layer).wait()
         mapped_here = mm(norm, xbc_w[layer]).astype(bf16)
         mapped[...] = mapped_here
 
@@ -155,7 +193,9 @@
 
         norm_seq = mm(perm[...], norm).astype(bf16)
         normed_seq[...] = norm_seq
-        raw = mm(norm_seq, step_w[layer]) + land_seq * of_layer(shift, layer)
+        raw = lax.dot_general(
+            norm_seq, step_w[layer], (((1,), (1,)), ((), ())), preferred_element_type=f32
+        ) + land_seq * of_layer(shift, layer)
         dt = jnp.maximum(raw, 0.0) + jnp.log1p(jnp.exp(-jnp.abs(raw)))
         log_step = -of_layer(rates, layer) * dt + reset_col * jnp.log(of_layer(keeps, layer))
         lower = ((rows >= cols) & (rows // Q == cols // Q)).astype(f32)
@@ -201,8 +241,7 @@
         at_first = (place_rows == place_cols * across).astype(f32).astype(bf16)
         at_last = (place_rows == place_cols * across + across - 1).astype(f32).astype(bf16)
 
-        @pl.loop(0, xbc_w.shape[2] // group)
-        def _(part):
+        def filter_part(part):
             lanes = pl.ds(pl.multiple_of(part * group, group), group)
             mid = mapped[:, lanes].astype(f32).reshape(lat, across, group)
             column = iota((lat, across, group), 1)
@@ -217,7 +256,11 @@
             for row_off in range(3):
                 line = None
                 for col_off, moved in enumerate((before, mid, after)):
-                    factor = conv_w[layer, row_off, pl.ds(col_off, 1), lanes]
+                    factor = jnp.where(
+                        layer == 0,
+                        conv_w[row_off, col_off, 0:1, lanes],
+                        conv_w[row_off, col_off, 1:2, lanes],
+                    )
                     term = moved * factor[None]
                     line = term if line is None else line + term
                 if row_off == 0:
@@ -229,34 +272,34 @@
                 (total * (1.0 / (1.0 + jnp.exp(-total)))).reshape(cells, group).astype(bf16)
             )
 
-        seq[...] = mm(perm[...], act[...]).astype(bf16)
-
-        x0, x1 = seq[0:Q, 0:E].astype(f32), seq[Q:, 0:E].astype(f32)
-        wx0 = (x0 * wide[0, 0:Q]).astype(bf16)
-        wx1 = (x1 * wide[0, Q:]).astype(bf16)
-        b0, b1 = seq[0:Q, E : E + N], seq[Q:, E : E + N]
-        b0_t = b0.astype(f32).T.astype(bf16)
-        b1_t = b1.astype(f32).T.astype(bf16)
-        first_added = mm(b0_t, wx0)
-        added0[...] = first_added.astype(bf16)
-        summary = (first_added * wide[1, 2 * Q - 1 : 2 * Q] + mm(b1_t, wx1)).astype(bf16)
-        for chunk in range(chunks):
-            r, c = chunk // per_row * 16, chunk % per_row * width
-            s_out[chunk] = summary[r : r + 16, c : c + width]
-
-        @pl.loop(1, tiles)
-        def _(step):
-            peer = lax.rem(me + step, tiles)
-
-            @pl.when(peer < chunks)
-            def _():
+        pl.loop(E // group, xbc_w.shape[2] // group)(filter_part)
+        seq[:, E:] = mm(perm[...], act[:, E:]).astype(bf16)
+        b0_t = seq[0:Q, E : E + N].astype(f32).T.astype(bf16)
+        b1_t = seq[Q:, E : E + N].astype(f32).T.astype(bf16)
+
+        for part in range(2):
+            lanes = slice(part * half, (part + 1) * half)
+            pl.loop(part * (half // group), (part + 1) * (half // group))(filter_part)
+            x_seq = mm(perm[...], act[:, lanes])
+            seq[:, lanes] = x_seq.astype(bf16)
+            wx = (x_seq * wide[0, :, lanes]).astype(bf16)
+            first_added = mm(b0_t, wx[0:Q])
+            added0[:, lanes] = first_added.astype(bf16)
+            summary = first_added * wide[1, 2 * Q - 1 : 2 * Q, lanes] + mm(b1_t, wx[Q:])
+            s_out[part] = summary.astype(bf16).reshape(team, owned, half)
+
+            @pl.loop(1, team)
+            def _(step):
+                peer = lax.rem(place + step, team)
                 remote(
-                    s_out.at[peer],
-                    s_in.at[layer, me],
-                    s_send.at[step],
-                    s_recv.at[layer, me],
-                    peer,
+                    s_out.at[part, peer],
+                    s_in.at[layer, part, place],
+                    s_send.at[part, step],
+                    s_recv.at[layer, part, place],
+                    base + peer,
                 ).start()
+
+            s_in[layer, part, place] = s_out[part, place]
 
         scores = [
             lax.dot_general(
@@ -288,95 +331,172 @@
                 y[span, lanes] = mm(jnp.concatenate(mixes, axis=1), both)
             return carry
 
-        lax.fori_loop(0, PAIRS // 2, pair_step, tuple(scores))
+        lax.fori_loop(0, PAIRS, pair_step, tuple(scores))
 
         @pl.loop(1, tiles)
         def _(step):
             source = lax.rem(me + tiles - step, tiles)
-            remote(d_out, d_in.at[layer, source], d_send.at[step], d_recv.at[layer, source], left).wait()
-
-        @pl.when(me < chunks)
-        def _():
-            s_in[layer, me] = s_out[me]
-            offset = lax.rem(me, per_row) * (width // P_SIZE)
-            pick = (
-                (iota((N, width), 0) == iota((N, width), 1) // P_SIZE + offset)
-                .astype(f32)
-                .astype(bf16)
+            remote(
+                d_out, d_in.at[layer, source], d_send.at[step], d_recv.at[layer, source], left
+            ).wait()
+
+        pick = (iota((N, E), 0) == iota((N, E), 1) // P_SIZE).astype(f32).astype(bf16)
+        high, low = split(d_in[layer].reshape(tiles * 8, N))
+        d_wide[...] = (mm(high, pick) + mm(low, pick)).reshape(tiles, 8, E)
+
+        def hand_back(part, tile):
+            return remote(
+                p_out.at[part, tile],
+                p_in.at[layer, part, place],
+                p_send.at[part, tile],
+                p_recv.at[layer, part, place],
+                base + tile,
             )
-            high, low = split(d_in[layer].reshape(tiles * 8, N))
-            d_wide[...] = (mm(high, pick) + mm(low, pick)).reshape(tiles, 8, width)
-
-            def tile_step(tile, state):
-                p_out[tile] = state.astype(bf16)
-
-                @pl.when(tile != me)
+
+        def total_copy(part, to):
+            return remote(
+                t_out.at[part],
+                t_in.at[layer, part, my_team],
+                t_send.at[part, to],
+                t_recv.at[layer, part, my_team],
+                to * team + place,
+            )
+
+        def keep_back(part):
+            p_in[layer, part, place] = p_out[part, place]
+
+        for part in range(2):
+            lanes = slice(part * half, (part + 1) * half)
+
+            def tile_step(tile, carry):
+                state, factor = carry
+                rel[part, tile] = state
+                factors[part, tile] = factor
+
+                @pl.when(my_team == 0)
+                def _():
+                    p_out[part, tile] = state.astype(bf16)
+
+                    @pl.when(tile != place)
+                    def _():
+                        hand_back(part, tile).start()
+
+                @pl.when(tile != place)
                 def _():
                     remote(
-                        p_out.at[tile],
-                        p_in.at[layer, me],
-                        p_send.at[tile],
-                        p_recv.at[layer, me],
-                        tile,
-                    ).start()
-                    remote(
-                        s_out.at[0], s_in.at[layer, tile], s_send.at[0], s_recv.at[layer, tile], left
+                        s_out.at[part, 0],
+                        s_in.at[layer, part, tile],
+                        s_send.at[part, 0],
+                        s_recv.at[layer, part, tile],
+                        left,
                     ).wait_recv()
 
-                return state * d_wide[tile, 0:1, :] + s_in[layer, tile].astype(f32)
-
-            lax.fori_loop(0, tiles, tile_step, jnp.zeros((16, width), f32))
-            p_in[layer, me] = p_out[me]
-
-        lax.fori_loop(PAIRS // 2, PAIRS, pair_step, tuple(scores))
+                decay = d_wide[base + tile, :, lanes]
+                return (
+                    state * decay[0:1] + s_in[layer, part, tile].astype(f32),
+                    factor * decay,
+                )
+
+            state, _ = lax.fori_loop(
+                0, team, tile_step, (jnp.zeros((owned, half), f32), jnp.ones((8, half), f32))
+            )
+            t_out[part] = state.astype(bf16)
+
+            @pl.loop(my_team + 1, teams)
+            def _(to):
+                total_copy(part, to).start()
+
+        fetch_weight(5, layer).wait()
         gate = mm(normed_seq[...], gate_w[layer]).astype(bf16).astype(f32)
         gates[...] = gate * (1.0 / (1.0 + jnp.exp(-gate)))
         y[...] += skip_wide * seq[:, 0:E].astype(f32)
         y[Q:, :] += wide[1, Q:] * mm(seq[Q:, E + N :], added0[...])
 
-        @pl.loop(0, chunks)
-        def _(source):
-            @pl.when(source != me)
+        for part in range(2):
+            lanes = slice(part * half, (part + 1) * half)
+
+            @pl.when(my_team > 0)
             def _():
+                def team_step(earlier, state):
+                    remote(
+                        t_out.at[part],
+                        t_in.at[layer, part, earlier],
+                        t_send.at[part, 0],
+                        t_recv.at[layer, part, earlier],
+                        left,
+                    ).wait_recv()
+                    decay = lax.fori_loop(
+                        0,
+                        team,
+                        lambda tile, so_far: so_far * d_wide[earlier * team + tile, :, lanes],
+                        jnp.ones((8, half), f32),
+                    )
+                    return state * decay[0:1] + t_in[layer, part, earlier].astype(f32)
+
+                entering = lax.fori_loop(
+                    0, my_team, team_step, jnp.zeros((owned, half), f32)
+                )
+
+                @pl.loop(0, team)
+                def _(tile):
+                    p_out[part, tile] = (
+                        entering * factors[part, tile, 0:1, :] + rel[part, tile]
+                    ).astype(bf16)
+
+                    @pl.when(tile != place)
+                    def _():
+                        hand_back(part, tile).start()
+
+            keep_back(part)
+
+        maps_seq = seq[:, E + N :]
+        for part in range(2):
+            lanes = slice(part * half, (part + 1) * half)
+
+            @pl.loop(1, team)
+            def _(step):
+                source = lax.rem(place + step, team)
                 remote(
-                    p_out.at[0], p_in.at[layer, source], p_send.at[0], p_recv.at[layer, source], left
+                    p_out.at[part, 0],
+                    p_in.at[layer, part, source],
+                    p_send.at[part, 0],
+                    p_recv.at[layer, part, source],
+                    left,
                 ).wait_recv()
 
-        entering = jnp.concatenate(
-            [
-                jnp.concatenate([p_in[layer, r * per_row + c] for c in range(per_row)], axis=1)
-                for r in range(N // 16)
-            ],
-            axis=0,
-        )
-        result = y[...] + wide[2] * mm(seq[:, E + N :], entering)
+            y[:, lanes] += wide[2, :, lanes] * mm(maps_seq, p_in[layer, part].reshape(N, half))
+
+        result = y[...]
         gated = result * gates[...]
         gated = (
             gated
             * lax.rsqrt(jnp.mean(gated * gated, axis=-1, keepdims=True) + epsilon)
             * of_layer(gain, layer)
         ).astype(bf16)
+        fetch_weight(13, layer).wait()
         back = mm(perm_t[...], gated).astype(bf16)
         stream[...] = (stream[...] + mm(back, out_w[layer])).astype(bf16).astype(f32)
 
         to_left.wait_send()
         to_right.wait_send()
 
-        @pl.loop(1, tiles)
-        def _(step):
-            peer = lax.rem(me + step, tiles)
-
-            @pl.when(peer < chunks)
-            def _():
+        for part in range(2):
+
+            @pl.loop(1, team)
+            def _(step):
+                peer = lax.rem(place + step, team)
                 remote(
-                    s_out.at[peer], s_in.at[layer, me], s_send.at[step], s_recv.at[layer, me], peer
+                    s_out.at[part, peer],
+                    s_in.at[layer, part, place],
+                    s_send.at[part, step],
+                    s_recv.at[layer, part, place],
+                    base + peer,
                 ).wait_send()
-
-            @pl.when(me < chunks)
-            def _():
-                remote(
-                    p_out.at[peer], p_in.at[layer, me], p_send.at[peer], p_recv.at[layer, me], peer
-                ).wait_send()
+                hand_back(part, peer).wait_send()
+
+            @pl.loop(my_team + 1, teams)
+            def _(to):
+                total_copy(part, to).wait_send()
 
     out[...] = stream[...].reshape(lat, across, channels).astype(bf16)
 
@@ -401,20 +521,38 @@
     lat, across, channels = fields.shape
     cells = lat * across
     mapped_width = xbc_weight.shape[2]
-    width = max(128, 8 * E // tiles)
-    chunks = N // 16 * (E // width)
+    team = min(8, tiles)
+    teams, owned, half = tiles // team, N // team, E // 2
     dma = pltpu.SemaphoreType.DMA
     vmem = pltpu.VMEM
+    arrays = (
+        fields,
+        order,
+        resets,
+        land.T,
+        xbc_weight,
+        gate_weight,
+        step_weight.transpose(0, 2, 1),
+        conv_weight.transpose(1, 2, 0, 3),
+        land_shift,
+        rates,
+        keeps,
+        skip_gain,
+        norm_gain,
+        out_weight,
+    )
     return pl.pallas_call(
-        functools.partial(kernel, tiles, chunks, width),
+        functools.partial(kernel, tiles, team),
         out_shape=jax.ShapeDtypeStruct(fields.shape, bf16),
-        in_specs=[pl.BlockSpec(memory_space=vmem)] * 14,
+        in_specs=[pl.BlockSpec(memory_space=pltpu.HBM)] * len(arrays),
         out_specs=pl.BlockSpec(memory_space=vmem),
-        scratch_shapes=[
+        scratch_shapes=[vmem(array.shape, array.dtype) for array in arrays]
+        + [
+            dma((len(arrays),)),
+            dma((3, LAYERS)),
             vmem((cells, channels), f32),
             vmem((cells, cells), bf16),
             vmem((cells, cells), bf16),
-            vmem((cells, channels), bf16),
             vmem((cells, mapped_width), bf16),
             vmem((cells, mapped_width), bf16),
             vmem((cells, mapped_width), bf16),
@@ -427,44 +565,35 @@
             vmem((N, E), bf16),
             vmem((2, lat, mapped_width), bf16),
             vmem((LAYERS, 2, lat, mapped_width), bf16),
-            vmem((chunks, 16, width), bf16),
-            vmem((LAYERS, tiles, 16, width), bf16),
+            vmem((2, team, owned, half), bf16),
+            vmem((LAYERS, 2, team, owned, half), bf16),
+            vmem((2, owned, half), bf16),
+            vmem((LAYERS, 2, teams, owned, half), bf16),
+            vmem((2, team, owned, half), f32),
+            vmem((2, team, 8, half), f32),
             vmem((8, N), f32),
             vmem((LAYERS, tiles, 8, N), f32),
-            vmem((tiles, 8, width), f32),
-            vmem((tiles, 16, width), bf16),
-            vmem((LAYERS, chunks, 16, width), bf16),
+            vmem((tiles, 8, E), f32),
+            vmem((2, team, owned, half), bf16),
+            vmem((LAYERS, 2, team, owned, half), bf16),
             dma((2,)),
             dma((LAYERS, 2)),
+            dma((2, team)),
+            dma((LAYERS, 2, team)),
+            dma((2, teams)),
+            dma((LAYERS, 2, teams)),
             dma((tiles,)),
             dma((LAYERS, tiles)),
-            dma((tiles,)),
-            dma((LAYERS, tiles)),
-            dma((tiles,)),
-            dma((LAYERS, chunks)),
+            dma((2, team)),
+            dma((LAYERS, 2, team)),
         ],
         compiler_params=pltpu.CompilerParams(
-            collective_id=0, has_side_effects=True, vmem_limit_bytes=48 * 1024 * 1024
+            collective_id=0, has_side_effects=True, vmem_limit_bytes=60 * 1024 * 1024
         ),
         cost_estimate=pl.CostEstimate(
             flops=2 * 10**9, bytes_accessed=8 * 10**6, transcendentals=3 * 10**6
         ),
-    )(
-        fields,
-        order,
-        resets,
-        land.reshape(1, cells),
-        xbc_weight,
-        gate_weight,
-        step_weight,
-        conv_weight,
-        land_shift,
-        rates,
-        keeps,
-        skip_gain,
-        norm_gain,
-        out_weight,
-    )
+    )(*arrays)
 
 
 def solution(mesh):

time: 66.1 us -> 49.5 us (0.75)
  local copies, waits for them, and re-layouts: 12.3 us -> 1.67 us
  Pallas kernels: 53.2 us -> 47.6 us
    unnamed x24 -> x1, local copies, waits for them, and re-layouts: 12.2 us -> 1.67 us
    pallas_call x1, Pallas kernels: 53.2 us -> 47.6 us  [shards(): pl.pallas_call(functools.partial(kernel, tiles, team), out_shape=jax.Shap...]
where the time goes in v2:
time: 49.5 us; the launch traced here: 49.3 us
  Pallas kernels  47.6 us (96%)
  local copies, waits for them, and re-layouts  1.67 us (3%)
    pallas_call x1, Pallas kernels, shards(): pl.pallas_call(functools.partial(kernel, tiles, team), out_shape=jax.Shap...  47.6 us
    unnamed x1, local copies, waits for them, and re-layouts  1.67 us

profile of v2, /device:TPU:17, one launch (start us, length us, event | category | flops | bytes accessed | tf_op | source)
XLA Modules:
  0.0 49.3 jit_solution(17720751409210750974)
XLA Ops:
  0.0 47.6 %shard_map.136 = bf16[32,8,512]{2,1,0:T(8,128)(2,1)} custom-call(bf16[32,8,512]{2,1,0:T(8,128)(2,1)} %refs_0_.1, s32[1,256]{1,0:T(1,128)} %refs_1_.1, s32[1,256]{1,0:T(1,128)} %refs_2_.1, s32[8,32]{1,0:T(8,128)} %bitcast.5, bf16[2,512,1280]{2,1,0:T(8,128)(2,1)} %refs_4_.1, bf16[2,512,1024]{2,1,0:T(8,128)(2,1)} %refs_5_.1, bf16[2,16,512]{2,1,0:T(8,128)(2,1)} %bitcast.4, ...), custom_call_target="tpu_custom_call" | custom-call | flops 2000000000 | bytes 8000000 | tf_op jit(solution)/shard_map/pallas_call | solution.py:544
  47.7 1.7 %copy.16 = bf16[32,8,512]{2,1,0:T(8,128)(2,1)} copy(bf16[32,8,512]{2,1,0:T(8,128)(2,1)} %shard_map.136) | data formatting | bytes 524288

commit v3 on v2

--- a/solution.py
+++ b/solution.py
@@ -28,6 +28,10 @@
     high = values.astype(bf16)
     low = (values - high.astype(f32)).astype(bf16)
     return high, low
+
+
+def silu(x):
+    return 0.5 * x * (1.0 + jnp.tanh(0.5 * x))
 
 
 def of_layer(ref, layer):
@@ -72,6 +76,8 @@
     t_in,
     rel,
     factors,
+    g_out,
+    g_in,
     d_out,
     d_in,
     d_wide,
@@ -83,6 +89,8 @@
     s_recv,
     t_send,
     t_recv,
+    g_send,
+    g_recv,
     d_send,
     d_recv,
     p_send,
@@ -121,14 +129,21 @@
 
     barrier = pltpu.get_barrier_semaphore()
 
-    @pl.loop(1, tiles)
+    def greet(device):
+        pl.semaphore_signal(
+            barrier, inc=1, device_id={"lon": device}, device_id_type=pl.DeviceIdType.MESH
+        )
+
+    greet(left)
+    greet(right)
+
+    @pl.loop(1, team)
     def _(step):
-        pl.semaphore_signal(
-            barrier,
-            inc=1,
-            device_id={"lon": lax.rem(me + step, tiles)},
-            device_id_type=pl.DeviceIdType.MESH,
-        )
+        greet(base + lax.rem(place + step, team))
+
+    @pl.loop(1, teams)
+    def _(step):
+        greet(lax.rem(my_team + step, teams) * team + place)
 
     for index in early:
         fetch(index).wait()
@@ -155,7 +170,6 @@
     for index in small:
         if index not in early:
             fetch(index).wait()
-    pl.semaphore_wait(barrier, tiles - 1)
 
     def remote(src, dst, send, recv, peer):
         return pltpu.make_async_remote_copy(
@@ -174,14 +188,15 @@
             values * lax.rsqrt(jnp.mean(values * values, axis=-1, keepdims=True) + epsilon)
         ).astype(bf16)
         fetch_weight(4, layer).wait()
-        mapped_here = mm(norm, xbc_w[layer]).astype(bf16)
-        mapped[...] = mapped_here
-
-        edge_rows, edge_cols = iota((lat, cells), 0), iota((lat, cells), 1)
-        first = (edge_cols == edge_rows * across).astype(f32).astype(bf16)
-        last = (edge_cols == edge_rows * across + across - 1).astype(f32).astype(bf16)
-        halo_out[0] = mm(first, mapped_here).astype(bf16)
-        halo_out[1] = mm(last, mapped_here).astype(bf16)
+        edge_rows, edge_cols = iota((2 * lat, cells), 0), iota((2 * lat, cells), 1)
+        edge_cell = edge_rows * across + jnp.where(edge_rows < lat, 0, across - 1 - cells)
+        edges = mm((edge_cols == edge_cell).astype(f32).astype(bf16), norm).astype(bf16)
+        halo_out[...] = mm(edges, xbc_w[layer]).astype(bf16).reshape(2, lat, -1)
+
+        @pl.when(layer == 0)
+        def _():
+            pl.semaphore_wait(barrier, team + teams)
+
         to_left = remote(
             halo_out.at[0], halo_in.at[layer, 1], halo_send.at[0], halo_recv.at[layer, 1], left
         )
@@ -190,6 +205,7 @@
         )
         to_left.start()
         to_right.start()
+        mapped[...] = mm(norm, xbc_w[layer]).astype(bf16)
 
         norm_seq = mm(perm[...], norm).astype(bf16)
         normed_seq[...] = norm_seq
@@ -211,17 +227,17 @@
         d_out[...] = jnp.zeros_like(d_out)
         d_out[:, 0:H] = jnp.broadcast_to(jnp.exp(cum0 + cum1), (8, H))
 
-        @pl.loop(1, tiles)
+        @pl.loop(1, team)
         def _(step):
             remote(
                 d_out,
-                d_in.at[layer, me],
+                d_in.at[layer, place],
                 d_send.at[step],
-                d_recv.at[layer, me],
-                lax.rem(me + step, tiles),
+                d_recv.at[layer, place],
+                base + lax.rem(place + step, team),
             ).start()
 
-        d_in[layer, me] = d_out[...]
+        d_in[layer, place] = d_out[...]
 
         weight = jnp.exp(jnp.where(second, cum1, cum0) - cum) * dt
         since = jnp.exp(cum)
@@ -269,7 +285,7 @@
                     line = jnp.concatenate([line[1:], empty], axis=0)
                 total = line if total is None else total + line
             act[:, lanes] = (
-                (total * (1.0 / (1.0 + jnp.exp(-total)))).reshape(cells, group).astype(bf16)
+                silu(total).reshape(cells, group).astype(bf16)
             )
 
         pl.loop(E // group, xbc_w.shape[2] // group)(filter_part)
@@ -333,16 +349,16 @@
 
         lax.fori_loop(0, PAIRS, pair_step, tuple(scores))
 
-        @pl.loop(1, tiles)
+        @pl.loop(1, team)
         def _(step):
-            source = lax.rem(me + tiles - step, tiles)
+            source = lax.rem(place + team - step, team)
             remote(
                 d_out, d_in.at[layer, source], d_send.at[step], d_recv.at[layer, source], left
             ).wait()
 
         pick = (iota((N, E), 0) == iota((N, E), 1) // P_SIZE).astype(f32).astype(bf16)
-        high, low = split(d_in[layer].reshape(tiles * 8, N))
-        d_wide[...] = (mm(high, pick) + mm(low, pick)).reshape(tiles, 8, E)
+        high, low = split(d_in[layer].reshape(team * 8, N))
+        d_wide[...] = (mm(high, pick) + mm(low, pick)).reshape(team, 8, E)
 
         def hand_back(part, tile):
             return remote(
@@ -362,6 +378,30 @@
                 to * team + place,
             )
 
+        def decay_copy(to):
+            return remote(
+                g_out,
+                g_in.at[layer, my_team],
+                g_send.at[to],
+                g_recv.at[layer, my_team],
+                to * team + place,
+            )
+
+        if teams > 2:
+            g_out[...] = functools.reduce(
+                lambda a, b: a * b, [d_in[layer, tile] for tile in range(team)]
+            )
+
+            @pl.loop(my_team + 1, teams)
+            def _(to):
+                decay_copy(to).start()
+
+            @pl.loop(0, my_team)
+            def _(earlier):
+                remote(
+                    g_out, g_in.at[layer, earlier], g_send.at[0], g_recv.at[layer, earlier], left
+                ).wait_recv()
+
         def keep_back(part):
             p_in[layer, part, place] = p_out[part, place]
 
@@ -372,14 +412,6 @@
                 state, factor = carry
                 rel[part, tile] = state
                 factors[part, tile] = factor
-
-                @pl.when(my_team == 0)
-                def _():
-                    p_out[part, tile] = state.astype(bf16)
-
-                    @pl.when(tile != place)
-                    def _():
-                        hand_back(part, tile).start()
 
                 @pl.when(tile != place)
                 def _():
@@ -391,7 +423,7 @@
                         left,
                     ).wait_recv()
 
-                decay = d_wide[base + tile, :, lanes]
+                decay = d_wide[tile, :, lanes]
                 return (
                     state * decay[0:1] + s_in[layer, part, tile].astype(f32),
                     factor * decay,
@@ -406,9 +438,19 @@
             def _(to):
                 total_copy(part, to).start()
 
+            @pl.when(my_team == 0)
+            def _():
+                @pl.loop(0, team)
+                def _(tile):
+                    p_out[part, tile] = rel[part, tile].astype(bf16)
+
+                    @pl.when(tile != place)
+                    def _():
+                        hand_back(part, tile).start()
+
         fetch_weight(5, layer).wait()
         gate = mm(normed_seq[...], gate_w[layer]).astype(bf16).astype(f32)
-        gates[...] = gate * (1.0 / (1.0 + jnp.exp(-gate)))
+        gates[...] = silu(gate)
         y[...] += skip_wide * seq[:, 0:E].astype(f32)
         y[Q:, :] += wide[1, Q:] * mm(seq[Q:, E + N :], added0[...])
 
@@ -425,13 +467,12 @@
                         t_recv.at[layer, part, earlier],
                         left,
                     ).wait_recv()
-                    decay = lax.fori_loop(
-                        0,
-                        team,
-                        lambda tile, so_far: so_far * d_wide[earlier * team + tile, :, lanes],
-                        jnp.ones((8, half), f32),
-                    )
-                    return state * decay[0:1] + t_in[layer, part, earlier].astype(f32)
+                    total = t_in[layer, part, earlier].astype(f32)
+                    if teams == 2:
+                        return total
+                    high, low = split(g_in[layer, earlier])
+                    decay = mm(high, pick[:, lanes]) + mm(low, pick[:, lanes])
+                    return state * decay[0:1] + total
 
                 entering = lax.fori_loop(
                     0, my_team, team_step, jnp.zeros((owned, half), f32)
@@ -479,6 +520,12 @@
 
         to_left.wait_send()
         to_right.wait_send()
+
+        if teams > 2:
+
+            @pl.loop(my_team + 1, teams)
+            def _(to):
+                decay_copy(to).wait_send()
 
         for part in range(2):
 
@@ -572,8 +619,10 @@
             vmem((2, team, owned, half), f32),
             vmem((2, team, 8, half), f32),
             vmem((8, N), f32),
-            vmem((LAYERS, tiles, 8, N), f32),
-            vmem((tiles, 8, E), f32),
+            vmem((LAYERS, teams, 8, N), f32),
+            vmem((8, N), f32),
+            vmem((LAYERS, team, 8, N), f32),
+            vmem((team, 8, E), f32),
             vmem((2, team, owned, half), bf16),
             vmem((LAYERS, 2, team, owned, half), bf16),
             dma((2,)),
@@ -582,8 +631,10 @@
             dma((LAYERS, 2, team)),
             dma((2, teams)),
             dma((LAYERS, 2, teams)),
-            dma((tiles,)),
-            dma((LAYERS, tiles)),
+            dma((teams,)),
+            dma((LAYERS, teams)),
+            dma((team,)),
+            dma((LAYERS, team)),
             dma((2, team)),
             dma((LAYERS, 2, team)),
         ],

time: 49.5 us -> 46.6 us (0.941)
  Pallas kernels: 47.6 us -> 44.7 us
    pallas_call x1, Pallas kernels: 47.6 us -> 44.7 us  [shards(): pl.pallas_call(functools.partial(kernel, tiles, team), out_shape=jax.Shap...]
where the time goes in v3:
time: 46.6 us; the launch traced here: 46.3 us
  Pallas kernels  44.7 us (96%)
  local copies, waits for them, and re-layouts  1.67 us (4%)
    pallas_call x1, Pallas kernels, shards(): pl.pallas_call(functools.partial(kernel, tiles, team), out_shape=jax.Shap...  44.7 us
    unnamed x1, local copies, waits for them, and re-layouts  1.67 us

profile of v3, /device:TPU:17, one launch (start us, length us, event | category | flops | bytes accessed | tf_op | source)
XLA Modules:
  0.0 46.3 jit_solution(17659893819693336977)
XLA Ops:
  0.0 44.7 %shard_map.136 = bf16[32,8,512]{2,1,0:T(8,128)(2,1)} custom-call(bf16[32,8,512]{2,1,0:T(8,128)(2,1)} %refs_0_.1, s32[1,256]{1,0:T(1,128)} %refs_1_.1, s32[1,256]{1,0:T(1,128)} %refs_2_.1, s32[8,32]{1,0:T(8,128)} %bitcast.5, bf16[2,512,1280]{2,1,0:T(8,128)(2,1)} %refs_4_.1, bf16[2,512,1024]{2,1,0:T(8,128)(2,1)} %refs_5_.1, bf16[2,16,512]{2,1,0:T(8,128)(2,1)} %bitcast.4, ...), custom_call_target="tpu_custom_call" | custom-call | flops 2000000000 | bytes 8000000 | tf_op jit(solution)/shard_map/pallas_call | solution.py:591
  44.7 1.7 %copy.16 = bf16[32,8,512]{2,1,0:T(8,128)(2,1)} copy(bf16[32,8,512]{2,1,0:T(8,128)(2,1)} %shard_map.136) | data formatting | bytes 524288

commit v4 on v3

--- a/solution.py
+++ b/solution.py
@@ -59,10 +59,10 @@
     perm,
     perm_t,
     mapped,
+    own_sum,
     act,
     seq,
     normed_seq,
-    gates,
     lt,
     dtt,
     y,
@@ -249,44 +249,60 @@
         skip_high, skip_low = split(jnp.broadcast_to(of_layer(skip, layer), (8, H)))
         skip_wide = (mm(skip_high, spread) + mm(skip_low, spread))[0:1]
 
-        to_left.wait_recv()
-        to_right.wait_recv()
-
         group = 256
-        place_rows, place_cols = iota((cells, lat), 0), iota((cells, lat), 1)
-        at_first = (place_rows == place_cols * across).astype(f32).astype(bf16)
-        at_last = (place_rows == place_cols * across + across - 1).astype(f32).astype(bf16)
-
-        def filter_part(part):
+
+        def taps(row_off, col_off, lanes):
+            return jnp.where(
+                layer == 0,
+                conv_w[row_off, col_off, 0:1, lanes],
+                conv_w[row_off, col_off, 1:2, lanes],
+            )
+
+        @pl.loop(0, xbc_w.shape[2] // group)
+        def _(part):
             lanes = pl.ds(pl.multiple_of(part * group, group), group)
             mid = mapped[:, lanes].astype(f32).reshape(lat, across, group)
             column = iota((lat, across, group), 1)
-            before = jnp.where(column == 0, 0.0, pltpu.roll(mid, 1, 1)) + mm(
-                at_first, halo_in[layer, 0, :, lanes]
-            ).reshape(lat, across, group)
-            after = jnp.where(column == across - 1, 0.0, pltpu.roll(mid, across - 1, 1)) + mm(
-                at_last, halo_in[layer, 1, :, lanes]
-            ).reshape(lat, across, group)
+            before = jnp.where(column == 0, 0.0, pltpu.roll(mid, 1, 1))
+            after = jnp.where(column == across - 1, 0.0, pltpu.roll(mid, across - 1, 1))
             total = None
             empty = jnp.zeros((1, across, group), f32)
             for row_off in range(3):
                 line = None
                 for col_off, moved in enumerate((before, mid, after)):
-                    factor = jnp.where(
-                        layer == 0,
-                        conv_w[row_off, col_off, 0:1, lanes],
-                        conv_w[row_off, col_off, 1:2, lanes],
-                    )
-                    term = moved * factor[None]
+                    term = moved * taps(row_off, col_off, lanes)[None]
                     line = term if line is None else line + term
                 if row_off == 0:
                     line = jnp.concatenate([empty, line[:-1]], axis=0)
                 if row_off == 2:
                     line = jnp.concatenate([line[1:], empty], axis=0)
                 total = line if total is None else total + line
-            act[:, lanes] = (
-                silu(total).reshape(cells, group).astype(bf16)
-            )
+            own_sum[:, lanes] = total.reshape(cells, group)
+
+        to_left.wait_recv()
+        to_right.wait_recv()
+
+        place_rows, place_cols = iota((cells, 4 * lat), 0), iota((cells, 4 * lat), 1)
+        target = place_cols % lat * across + jnp.where(place_cols < 2 * lat, 0, across - 1)
+        at_edges = (place_rows == target).astype(f32).astype(bf16)
+
+        def filter_part(part):
+            lanes = pl.ds(pl.multiple_of(part * group, group), group)
+            line_row = iota((lat, group), 0)
+            terms = []
+            for side in range(2):
+                edge = halo_in[layer, side, :, lanes].astype(f32)
+                above = jnp.where(line_row == 0, 0.0, pltpu.roll(edge, 1, 0))
+                below = jnp.where(line_row == lat - 1, 0.0, pltpu.roll(edge, lat - 1, 0))
+                terms.extend(
+                    split(
+                        above * taps(0, 2 * side, lanes)
+                        + edge * taps(1, 2 * side, lanes)
+                        + below * taps(2, 2 * side, lanes)
+                    )
+                )
+            total = own_sum[:, lanes] + mm(at_edges, jnp.concatenate(terms, axis=0))
+            act[:, lanes] = silu(total).astype(bf16)
 
         pl.loop(E // group, xbc_w.shape[2] // group)(filter_part)
         seq[:, E:] = mm(perm[...], act[:, E:]).astype(bf16)
@@ -450,9 +466,14 @@
 
         fetch_weight(5, layer).wait()
         gate = mm(normed_seq[...], gate_w[layer]).astype(bf16).astype(f32)
-        gates[...] = silu(gate)
-        y[...] += skip_wide * seq[:, 0:E].astype(f32)
-        y[Q:, :] += wide[1, Q:] * mm(seq[Q:, E + N :], added0[...])
+        gate = silu(gate)
+        wide[2] = wide[2] * gate
+        y[0:Q, :] = (y[0:Q, :] + skip_wide * seq[0:Q, 0:E].astype(f32)) * gate[0:Q]
+        y[Q:, :] = (
+            y[Q:, :]
+            + skip_wide * seq[Q:, 0:E].astype(f32)
+            + wide[1, Q:] * mm(seq[Q:, E + N :], added0[...])
+        ) * gate[Q:]
 
         for part in range(2):
             lanes = slice(part * half, (part + 1) * half)
@@ -507,8 +528,7 @@
 
             y[:, lanes] += wide[2, :, lanes] * mm(maps_seq, p_in[layer, part].reshape(N, half))
 
-        result = y[...]
-        gated = result * gates[...]
+        gated = y[...]
         gated = (
             gated
             * lax.rsqrt(jnp.mean(gated * gated, axis=-1, keepdims=True) + epsilon)
@@ -601,10 +621,10 @@
             vmem((cells, cells), bf16),
             vmem((cells, cells), bf16),
             vmem((cells, mapped_width), bf16),
+            vmem((cells, mapped_width), f32),
             vmem((cells, mapped_width), bf16),
             vmem((cells, mapped_width), bf16),
             vmem((cells, channels), bf16),
-            vmem((cells, E), f32),
             vmem((PAIRS, 2, cells), f32),
             vmem((PAIRS, 2, cells), f32),
             vmem((cells, E), f32),

time: 46.6 us -> 45.4 us (0.974)
  Pallas kernels: 44.7 us -> 43.5 us
    pallas_call x1, Pallas kernels: 44.7 us -> 43.5 us  [shards(): pl.pallas_call(functools.partial(kernel, tiles, team), out_shape=jax.Shap...]
where the time goes in v4:
time: 45.4 us; the launch traced here: 45.2 us
  Pallas kernels  43.5 us (96%)
  local copies, waits for them, and re-layouts  1.67 us (4%)
    pallas_call x1, Pallas kernels, shards(): pl.pallas_call(functools.partial(kernel, tiles, team), out_shape=jax.Shap...  43.5 us
    unnamed x1, local copies, waits for them, and re-layouts  1.67 us

profile of v4, /device:TPU:17, one launch (start us, length us, event | category | flops | bytes accessed | tf_op | source)
XLA Modules:
  0.0 45.2 jit_solution(5631517486180703296)
XLA Ops:
  0.0 43.5 %shard_map.136 = bf16[32,8,512]{2,1,0:T(8,128)(2,1)} custom-call(bf16[32,8,512]{2,1,0:T(8,128)(2,1)} %refs_0_.1, s32[1,256]{1,0:T(1,128)} %refs_1_.1, s32[1,256]{1,0:T(1,128)} %refs_2_.1, s32[8,32]{1,0:T(8,128)} %bitcast.5, bf16[2,512,1280]{2,1,0:T(8,128)(2,1)} %refs_4_.1, bf16[2,512,1024]{2,1,0:T(8,128)(2,1)} %refs_5_.1, bf16[2,16,512]{2,1,0:T(8,128)(2,1)} %bitcast.4, ...), custom_call_target="tpu_custom_call" | custom-call | flops 2000000000 | bytes 8000000 | tf_op jit(solution)/shard_map/pallas_call | solution.py:611
  43.6 1.7 %copy.16 = bf16[32,8,512]{2,1,0:T(8,128)(2,1)} copy(bf16[32,8,512]{2,1,0:T(8,128)(2,1)} %shard_map.136) | data formatting | bytes 524288
